TPU v7x, 32 devices: a whole 2x2x4 slice. The times are simulated.
32 devices in a mesh: section: 2 (over x), dp: 16 (over z, y, core).
Axes of the slice: x: 2, y: 2, z: 4, core: 2. Of those that a mesh axis runs over, the one named last changes fastest.
Arguments:
- cells_in: bfloat16 [32, 1024, 256], P('dp'), may hold values from -6 to 6
- out_grad: bfloat16 [32, 1024, 256], P('dp'), may hold values from -6 to 6
- segment_ids: int32 [32, 1024], P('dp'), may hold values from 0 to 11, never falling along the last dimension, each value on 1 to 512 neighbouring positions
- real_lengths: int32 [32], P('dp'), may hold values from 512 to 1024, as said below
- w_qkv: bfloat16 [2, 256, 768], P('section'), may hold values from -0.375 to 0.375
- w_attn_out: bfloat16 [2, 256, 256], P('section'), may hold values from -2 to 2
- w_up: bfloat16 [2, 256, 512], P('section'), may hold values from -0.375 to 0.375
- w_down: bfloat16 [2, 512, 256], P('section'), may hold values from -0.25 to 0.25
- norm_gains: float32 [2, 2, 256], P('section'), may hold values from 0.5 to 1.5
- biases: float32 [2, 6, 256], P('section'), may hold values from -3 to 3
- up_bias: float32 [2, 512], P('section'), may hold values from -3 to 3
Outputs:
- layer_out: bfloat16 [2, 32, 1024, 256], P('section', 'dp')
- input_grad: float32 [2, 32, 1024, 256], P('section', 'dp')
- grad_qkv: float32 [2, 256, 768], P('section')
- grad_attn_out: float32 [2, 256, 256], P('section')
- grad_up: float32 [2, 256, 512], P('section')
- grad_down: float32 [2, 512, 256], P('section')
- grad_gains: float32 [2, 2, 256], P('section')
- grad_biases: float32 [2, 6, 256], P('section')
- grad_up_bias: float32 [2, 512], P('section')
Inputs may be any that keep to these rules, and one draw needn't show every extreme that they name: segment_ids never fall along a row; the tokens of one cell share one number. The first real_lengths[r] tokens of row r are real, the rest padding.
All inputs are finite; a program needn't handle non-finite values.
Results may differ from a plain program's by a relative error of at most 0.013.
Values may be sent and summed in bfloat16 or wider, within the bound.
A program may use at most 192 MiB of HBM per device.

v0:
```python
import types

import jax
import jax.numpy as jnp
from jax import lax
from jax.experimental import pallas as pl
from jax.experimental.pallas import tpu as pltpu
from jax.sharding import PartitionSpec as P

MESH = pl.DeviceIdType.MESH
bf16 = jnp.bfloat16
f32 = jnp.float32
HEADS = 4
TILE = 256
REACH = 511
SEGMENTS = 12
CODE = 2.0**50
GELU_A = 0.7978845608028654
GELU_B = 0.044715


def dot(a, b):
    return lax.dot_general(a, b, (((1,), (0,)), ((), ())), preferred_element_type=f32)


def dot_tn(a, b):
    return lax.dot_general(a, b, (((0,), (0,)), ((), ())), preferred_element_type=f32)


def lanes(rows, width=128):
    return lax.broadcasted_iota(jnp.int32, (rows, width), 1)


def column_sum(v):
    return jnp.sum(v, axis=0, keepdims=True)


def setup(R):
    n = R.n
    token = lax.broadcasted_iota(jnp.int32, (64, n), 1)
    code = lax.broadcasted_iota(jnp.int32, (64, n), 0)
    segment = jnp.where(token < R.length, R.seg_row, SEGMENTS)
    used = code <= SEGMENTS
    key_code = jnp.where(used & (code == segment), CODE, 0.0).astype(bf16)
    query_code = jnp.where(used & (code != segment), -CODE, 0.0).astype(bf16)
    R.qcode[...] = jnp.concatenate([jnp.zeros((64, n), bf16), query_code], axis=0).T
    for h in range(HEADS):
        R.kc[128 * h + 64 : 128 * h + 128, :] = key_code
    R.vT[256:320, :] = jnp.zeros((64, n), bf16)


def spans(n):
    out = []
    for i in range(n // TILE):
        lo = max(0, (i * TILE - REACH) // 128 * 128)
        hi = min(n, -(-(i * TILE + TILE + REACH) // 128) * 128)
        out.append((lo, hi - lo))
    return out


def head_tile(pair, h):
    return pair if h % 2 == 0 else pltpu.roll(pair, 64, 1)


def real_rows(R, start, rows):
    return (start + lax.broadcasted_iota(jnp.int32, (rows, 1), 0)) < R.length


def pick_heads(t):
    lane = lanes(TILE, 256) // 64
    o = t[0:TILE]
    for h in range(1, HEADS):
        o = jnp.where(lane == h, t[h * TILE : h * TILE + TILE], o)
    return o


def project(R, l):
    n = R.n
    shift = jnp.concatenate([R.biases[l, 0], jnp.zeros((1, 256), f32), R.biases[l, 1]], axis=1)
    packed = dot(R.x[l], R.wqkv[l]) + shift
    lane = lanes(n)
    q = packed[:, 0:256] * 0.125
    R.qn[l] = q.astype(bf16)
    for h in range(HEADS):
        t = head_tile(q[:, 128 * (h // 2) : 128 * (h // 2) + 128], h)
        R.qh[h] = jnp.where(lane < 64, t, 0.0).astype(bf16) + R.qcode[...]
    k = packed[:, 256:512].astype(bf16)
    R.kn[l] = k
    R.vn[l] = packed[:, 512:768].astype(bf16)
    kT = k.T
    for h in range(HEADS):
        R.kc[128 * h : 128 * h + 64, :] = kT[64 * h : 64 * h + 64]


def attend_tile(R, l, i):
    lo, width = spans(R.n)[i]
    rows, cols = pl.ds(i * TILE, TILE), pl.ds(lo, width)
    real = real_rows(R, i * TILE, TILE)
    for h in range(HEADS):
        s = dot(R.qh[h, rows, :], R.kc[128 * h : 128 * h + 128, cols])
        e = jnp.exp(s - jnp.max(s, axis=1, keepdims=True))
        r = jnp.where(real, 1.0 / jnp.sum(e, axis=1, keepdims=True), 0.0)
        R.P[i][h * TILE : h * TILE + TILE, :] = (e * r).astype(bf16)
    o = pick_heads(dot(R.P[i][...], R.vn[l, cols, :]))
    o = jnp.where(real, o, R.vn[l, rows, :].astype(f32))
    R.octx[l, rows, :] = o


def norm(v):
    c = v - jnp.mean(v, axis=-1, keepdims=True)
    s = lax.rsqrt(jnp.mean(c * c, axis=-1, keepdims=True) + 1e-5)
    return c * s, s


def feed(R, l):
    att = dot(R.octx[l].astype(bf16), R.wout[l]) + R.biases[l, 2]
    n1, s1 = norm(R.x[l].astype(f32) + att)
    hidden = n1 * R.gains[l, 0:1] + R.biases[l, 3]
    low = hidden.astype(bf16)
    u = dot(low, R.wup[l]) + R.upb[l]
    q = (GELU_A * GELU_B) * (u * u)
    w = 0.5 * jnp.tanh(u * (q + GELU_A)) + 0.5
    a = u * w
    act = a.astype(bf16)
    slope = w + a * ((1.0 - w) * (6.0 * q + 2.0 * GELU_A))
    n2, s2 = norm(hidden + (dot(act, R.wdown[l]) + R.biases[l, 4]))
    R.n1[l] = n1
    R.stat[l, :, 4:5] = s1
    R.gp[l] = slope
    R.act[l] = act
    R.n2[l] = n2
    R.stat[l, :, 5:6] = s2
    R.x[l + 1] = (n2 * R.gains[l, 1:2] + R.biases[l, 5]).astype(bf16)


def norm_back(g, n, s, gain):
    gg = g * gain
    return s * (gg - jnp.mean(gg, axis=-1, keepdims=True) - n * jnp.mean(gg * n, axis=-1, keepdims=True))


def put_small(ref, row, v):
    ref[0, row : row + 1, :] = v[:, 0:128]
    ref[1, row : row + 1, :] = v[:, 128:256]


def feed_back(R, l, g):
    n = R.n
    R.woutT[...] = R.wout[l].T
    R.wupT[...] = R.wup[l].T
    R.wdownT[...] = R.wdown[l].T
    R.wqkvT[...] = R.wqkv[l].T
    small = R.small.at[l]
    n2 = R.n2[l]
    d2 = norm_back(g, n2, R.stat[l, :, 5:6], R.gains[l, 1:2])
    put_small(small, 1, column_sum(g * n2))
    put_small(small, 5, column_sum(g))
    dl = d2.astype(bf16)
    R.dlow[...] = dl
    put_small(small, 4, column_sum(d2))
    du = dot(dl, R.wdownT[...]) * R.gp[l]
    up = column_sum(du)
    put_small(small, 6, up[:, 0:256])
    put_small(small, 7, up[:, 256:512])
    du = du.astype(bf16)
    R.dup[...] = du
    dh = d2 + dot(du, R.wupT[...])
    n1 = R.n1[l]
    low = (n1 * R.gains[l, 0:1] + R.biases[l, 3]).astype(bf16)
    d1 = norm_back(dh, n1, R.stat[l, :, 4:5], R.gains[l, 0:1])
    put_small(small, 0, column_sum(dh * n1))
    put_small(small, 3, column_sum(dh))
    put_small(small, 2, column_sum(d1))
    R.d1[...] = d1
    da = d1.astype(bf16)
    R.datt[...] = da
    dcb = dot(da, R.woutT[...]).astype(bf16)
    R.dctx[...] = dcb
    dc = dcb.astype(f32)
    e = dc * R.octx[l]
    lane = lanes(n)
    for h in range(HEADS):
        pair = slice(128 * (h // 2), 128 * (h // 2) + 128)
        R.delta[:, h : h + 1] = jnp.sum(
            jnp.where((lane // 64) == (h % 2), e[:, pair], 0.0), axis=1, keepdims=True
        )
        R.doh[h] = jnp.where(lane < 64, head_tile(dc[:, pair], h), 0.0).astype(bf16)
    R.doT[...] = dcb.T
    R.qT[...] = R.qn[l].T
    R.vT[0:256, :] = R.vn[l].T
    R.grad_a[l, :, 0:256] = dot_tn(R.octx[l].astype(bf16), R.datt[...])
    R.grad_a[l, :, 256:768] = dot_tn(low, R.dup[...])
    R.grad_a[l, :, 768:1280] = dot_tn(R.dlow[...], R.act[l])
    R.dkT[...] = jnp.zeros_like(R.dkT)
    R.dvT[...] = jnp.zeros_like(R.dvT)


def attend_back_tile(R, l, i):
    lo, width = spans(R.n)[i]
    rows, cols = pl.ds(i * TILE, TILE), pl.ds(lo, width)
    for h in range(HEADS):
        head, part = slice(64 * h, 64 * h + 64), slice(h * TILE, h * TILE + TILE)
        p = R.P[i][part, :]
        dp = dot(R.doh[h, rows, :], R.vT[64 * h : 64 * h + 128, cols])
        R.DS[part, 0:width] = (p.astype(f32) * (dp - R.delta[rows, h : h + 1])).astype(bf16)
        R.dvT[head, cols] += dot(R.doT[head, rows], p)
    for h in range(HEADS):
        head, part = slice(64 * h, 64 * h + 64), slice(h * TILE, h * TILE + TILE)
        R.dkT[head, cols] += dot(R.qT[head, rows], R.DS[part, 0:width])
    R.dqkv[rows, 0:256] = (pick_heads(dot(R.DS[:, 0:width], R.kn[l, cols, :])) * 0.125).astype(bf16)


def project_back(R, l):
    real = real_rows(R, 0, R.n)
    dv = R.dvT[...].T + jnp.where(real, 0.0, R.dctx[...].astype(f32))
    R.dqkv[:, 256:512] = R.dkT[...].T.astype(bf16)
    R.dqkv[:, 512:768] = dv.astype(bf16)
    put_small(R.small.at[l], 8, column_sum(R.dqkv[:, 0:256].astype(f32)))
    put_small(R.small.at[l], 9, column_sum(dv))
    d = R.d1[...] + dot(R.dqkv[...], R.wqkvT[...])
    R.d1[...] = d
    R.dinb[l] = d.astype(bf16)


def weight_back(R, l):
    R.grad_b[l] = dot_tn(R.x[l], R.dqkv[...])


class Links:
    def __init__(self, dp, send, recv, local):
        self.sec = lax.axis_index("section")
        self.dp = lax.axis_index("dp")
        self.send, self.recv, self.local_sem = send, recv, local
        self.used = 0
        self.used_local = 0
        self.core = self.dp % 2
        self.chips = min(8, dp // 2)
        self.groups = dp // (2 * self.chips)
        self.chip = (self.dp // 2) % self.chips
        self.pending = []

    def flip(self, index, bit):
        return index + bit - 2 * bit * ((index // bit) % 2)

    def xor(self, index, mask):
        bit = 1
        while bit <= mask:
            if mask & bit:
                index = self.flip(index, bit)
            bit *= 2
        return index

    def section_peer(self):
        return (1 - self.sec, self.dp)

    def core_peer(self):
        return (self.sec, self.flip(self.dp, 1))

    def chip_peer(self, k):
        return (self.sec, self.xor(self.dp, 2 * k))

    def group_peer(self, k):
        return (self.sec, self.xor(self.dp, 2 * self.chips * k))

    def peers(self):
        out = [self.section_peer(), self.core_peer()]
        out += [self.chip_peer(k) for k in range(1, self.chips)]
        out += [self.group_peer(k) for k in range(1, self.groups)]
        return out

    def remote(self, src, dst, peer):
        i = self.used
        self.used += 1
        return pltpu.make_async_remote_copy(
            src, dst, self.send.at[i], self.recv.at[i], device_id=peer, device_id_type=MESH
        )

    def local(self, src, dst):
        i = self.used_local
        self.used_local += 1
        return pltpu.make_async_copy(src, dst, self.local_sem.at[i])


def reduction(K, l, grad, small, R, name):
    get = lambda part: getattr(R, name + "_" + part).at[l]
    r1, s2, r2, acc, r3, done = [get(p) for p in ("r1", "s2", "r2", "acc", "r3", "done")]
    res = getattr(R, "res_" + name)
    c, chip, chips, groups = K.core, K.chip, K.chips, K.groups
    half = grad.shape[0] // 2
    piece = half // chips
    mine = pl.ds(c * half, half)
    other = pl.ds((1 - c) * half, half)
    part = pl.ds(c * half + chip * piece, piece)
    owner = K.sec == l
    core_out = [K.remote(grad.at[other], r1, K.core_peer())]
    scatter = []
    for k in range(1, chips):
        there = K.xor(chip, k)
        scatter.append(K.remote(s2.at[pl.ds(there * piece, piece)], r2.at[k], K.chip_peer(k)))
    across = [K.remote(acc, r3, K.section_peer())]
    gather = [K.remote(done, res.at[part], K.chip_peer(k)) for k in range(1, chips)]
    keep = K.local(done, res.at[part])
    core_back = [K.remote(res.at[mine], res.at[mine], K.core_peer())]
    spread = []
    if groups > 1:
        r4 = get("r4")
        spread = [K.remote(acc, r4.at[k], K.group_peer(k)) for k in range(1, groups)]
    if small is not None:
        q1, q2, t2, qacc, q3, qres = [get(p) for p in ("q1", "q2", "t2", "qacc", "q3", "qres")]
        core_out.append(K.remote(small.at[1 - c], q1, K.core_peer()))
        scatter += [K.remote(q2, t2.at[k], K.chip_peer(k)) for k in range(1, chips)]
        across.append(K.remote(qacc, q3, K.section_peer()))
        core_back.append(K.remote(qres.at[c], qres.at[c], K.core_peer()))
        small_out = K.local(qres, R.small_out)
        if groups > 1:
            q4 = get("q4")
            spread += [K.remote(qacc, q4.at[k], K.group_peer(k)) for k in range(1, groups)]

    def begin():
        for x in core_out:
            x.start()

    def scatter_pieces():
        for x in core_out:
            x.wait()
        total = grad[mine, :] + r1[...]
        grad[mine, :] = total
        s2[...] = total.astype(bf16)
        if small is not None:
            q2[...] = small[c] + q1[...]
        for x in scatter:
            x.start()

    def sum_pieces():
        for x in scatter:
            x.wait()
        total = grad[part, :]
        for k in range(1, chips):
            total = total + r2[k].astype(f32)
        acc[...] = total
        if small is not None:
            little = q2[...]
            for k in range(1, chips):
                little = little + t2[k]
            qacc[...] = little

        @pl.when(jnp.logical_not(owner))
        def _():
            for x in across:
                x.start()
            for x in across:
                x.wait_send()

    def gather_pieces():
        @pl.when(owner)
        def _():
            for x in across:
                x.wait_recv()
            acc[...] += r3[...]
            if small is not None:
                qacc[...] += q3[...]
            for x in spread:
                x.start()
            for x in spread:
                x.wait()
            total = acc[...]
            for k in range(1, groups):
                total = total + r4[k]
            done[...] = total.astype(bf16)
            for x in gather:
                x.start()
            keep.start()
            if small is not None:
                little = qacc[...]
                for k in range(1, groups):
                    little = little + q4[k]
                qres[c] = little
                core_back[1].start()

    def share():
        @pl.when(owner)
        def _():
            for x in gather:
                x.wait()
            keep.wait()
            core_back[0].start()

    def finish():
        @pl.when(owner)
        def _():
            for x in core_back:
                x.wait()
            if small is not None:
                small_out.start()
                small_out.wait()

    return begin, scatter_pieces, sum_pieces, gather_pieces, share, finish


def scratch(n, chips, groups):
    def V(*s):
        return pltpu.VMEM(s[:-1], s[-1])

    out = dict(
        wqkv=V(2, 256, 768, bf16), wout=V(2, 256, 256, bf16), wup=V(2, 256, 512, bf16), wdown=V(2, 512, 256, bf16),
        gains=V(2, 2, 256, f32), biases=V(2, 6, 1, 256, f32), upb=V(2, 1, 512, f32),
        x=V(3, n, 256, bf16), qn=V(2, n, 256, bf16), kn=V(2, n, 256, bf16), vn=V(2, n, 256, bf16),
        octx=V(2, n, 256, f32), DS=V(HEADS * TILE, n, bf16),
        n1=V(2, n, 256, f32), n2=V(2, n, 256, f32), stat=V(2, n, 128, f32),
        gp=V(2, n, 512, f32), act=V(2, n, 512, bf16),
        qcode=V(n, 128, bf16), qh=V(HEADS, n, 128, bf16), kc=V(512, n, bf16), vT=V(320, n, bf16),
        doh=V(HEADS, n, 128, bf16), doT=V(256, n, bf16), qT=V(256, n, bf16), delta=V(n, 128, f32), dctx=V(n, 256, bf16),
        dkT=V(256, n, f32), dvT=V(256, n, f32), dqkv=V(n, 768, bf16),
        d1=V(n, 256, f32),
        woutT=V(256, 256, bf16), wupT=V(512, 256, bf16), wdownT=V(256, 512, bf16), wqkvT=V(768, 256, bf16),
        dinb=V(2, n, 256, bf16),
        small=V(2, 2, 16, 128, f32),
    )
    for name, width in (("a", 1280), ("b", 768)):
        piece = 128 // chips
        out["grad_" + name] = V(2, 256, width, f32)
        out[name + "_r1"] = V(2, 128, width, f32)
        out[name + "_s2"] = V(2, 128, width, bf16)
        out[name + "_r2"] = V(2, chips, piece, width, bf16)
        out[name + "_acc"] = V(2, piece, width, f32)
        out[name + "_r3"] = V(2, piece, width, f32)
        out[name + "_done"] = V(2, piece, width, bf16)
        if groups > 1:
            out[name + "_r4"] = V(2, groups, piece, width, f32)
    for part, lead in (("q1", ()), ("q2", ()), ("t2", (chips,)), ("qacc", ()), ("q3", ()), ("qres", (2,)), ("q4", (groups,))):
        out["b_" + part] = V(2, *lead, 16, 128, f32)
    for i, (_, width) in enumerate(spans(n)):
        out["P%d" % i] = V(HEADS * TILE, width, bf16)
    copies = 32 + 4 * (8 + 3 * chips + 2 * groups)
    out["send"] = pltpu.SemaphoreType.DMA((copies,))
    out["recv"] = pltpu.SemaphoreType.DMA((copies,))
    out["local"] = pltpu.SemaphoreType.DMA((64,))
    return out


INS = ["len_s", "seg_v", "cells", "ograd", "i_wqkv", "i_wout", "i_wup", "i_wdown", "i_gains", "i_biases", "i_upb"]
OUTS = ["layer_out", "din_own", "rdin", "res_a", "res_b", "small_out"]
WEIGHTS = ["wqkv", "wout", "wup", "wdown", "gains", "biases", "upb"]


def body(R, n, dp):
    K = Links(dp, R.send, R.recv, R.local)
    sec, c = K.sec, K.core
    R.n = n
    R.P = [getattr(R, "P%d" % i) for i in range(n // TILE)]
    R.dup = R.DS.at[:, pl.ds(0, 512)]
    R.dlow = R.DS.at[:, pl.ds(512, 256)]
    R.datt = R.DS.at[:, pl.ds(768, 256)]
    R.length = R.len_s[sec]
    R.seg_row = R.seg_v[pl.ds(sec, 1), :]

    barrier = pltpu.get_barrier_semaphore()
    peers = K.peers()
    for peer in peers:
        pl.semaphore_signal(barrier, 1, device_id=peer, device_id_type=MESH)

    take_x = K.local(R.cells.at[sec], R.x.at[0])
    take_g = K.local(R.ograd.at[sec], R.dinb.at[0])
    given = {w: getattr(R, "i_" + w) if w == "biases" else getattr(R, "i_" + w).at[0] for w in WEIGHTS}
    own = [K.local(given[w], getattr(R, w).at[sec]) for w in WEIGHTS]
    take_x.start()
    for x in own:
        x.start()
    take_g.start()

    away, forward_on = {}, {}
    for w in WEIGHTS:
        src, slots = given[w], getattr(R, w)
        if w in ("gains", "biases", "upb"):
            away[w] = K.remote(src, slots.at[sec], K.section_peer())
        else:
            half = src.shape[0] // 2
            rows = pl.ds(c * half, half)
            away[w] = K.remote(src.at[rows], slots.at[sec, rows], K.section_peer())
            theirs = slots.at[1 - sec, rows]
            forward_on[w] = K.remote(theirs, theirs, K.core_peer())

    setup(R)
    pl.semaphore_wait(barrier, len(peers))
    first = ("biases", "wqkv")
    second = ("gains", "upb", "wout", "wup", "wdown")
    for w in first + second:
        away[w].start()
    take_x.wait()
    for x in own:
        x.wait()

    def take_first():
        for w in first:
            away[w].wait()
        forward_on["wqkv"].start()

    @pl.when(sec == 1)
    def _():
        take_first()
        forward_on["wqkv"].wait()

    n_tiles = n // TILE
    x_out = [
        (K.local(R.x.at[l + 1], R.layer_out.at[sec]), K.remote(R.x.at[l + 1], R.layer_out.at[sec], K.section_peer()))
        for l in range(2)
    ]

    def start_out(l, pair):
        pl.when(sec == l)(pair[0].start)
        pl.when(sec != l)(pair[1].start)

    stash = [getattr(R, "stash%d" % i) for i in range(n_tiles)]
    put_away = [K.local(R.P[i], stash[i]) for i in range(n_tiles)]
    bring_back = [K.local(stash[i], R.P[i]) for i in range(n_tiles)]

    def starts(copies):
        for x in copies:
            x.start()

    def waits(copies):
        for x in copies:
            x.wait()

    def forward(l, _):
        def at(layer, *steps):
            @pl.when(l == layer)
            def _():
                for step in steps:
                    step()

        project(R, l)
        at(1, lambda: waits(put_away))
        for i in range(n_tiles):
            attend_tile(R, l, i)
            if i == n_tiles - 2:
                at(
                    0,
                    lambda: starts(put_away[: n_tiles - 1]),
                    lambda: pl.when(sec == 0)(take_first),
                    lambda: waits([away[w] for w in second]),
                    lambda: starts([forward_on[w] for w in ("wout", "wup", "wdown")]),
                )
        at(0, lambda: starts(put_away[n_tiles - 1 :]), lambda: waits([forward_on[w] for w in ("wout", "wup", "wdown")]),
            lambda: pl.when(sec == 0)(forward_on["wqkv"].wait))
        feed(R, l)
        at(0, lambda: start_out(0, x_out[0]))
        at(1, lambda: start_out(1, x_out[1]))
        return 0

    lax.fori_loop(0, 2, forward, 0)

    R.small[...] = jnp.zeros_like(R.small)
    A = [reduction(K, l, R.grad_a.at[l], None, R, "a") for l in range(2)]
    B = [reduction(K, l, R.grad_b.at[l], R.small.at[l], R, "b") for l in range(2)]
    BEGIN, SCATTER, SUM, GATHER, SHARE, FINISH = range(6)

    din_local = [K.local(R.d1, R.din_own) for l in range(2)]
    quarter = n // 4
    din_away = [
        K.remote(R.dinb.at[1], R.rdin, K.section_peer()),
        [K.remote(R.dinb.at[0, pl.ds(i * quarter, quarter)], R.rdin.at[pl.ds(i * quarter, quarter)], K.section_peer()) for i in range(4)],
    ]
    take_g.wait()

    def start_din(l, part=slice(None)):
        @pl.when(sec == l)
        def _():
            din_local[l].start()

        @pl.when(sec != l)
        def _():
            starts([din_away[0]] if l == 1 else din_away[1][:2])

    def backward(j, _):
        l = 1 - j

        def at(turn, *steps):
            @pl.when(j == turn)
            def _():
                for step in steps:
                    step()

        at(1, lambda: pl.when(sec == 1)(din_local[1].wait))
        feed_back(R, l, R.dinb[j].astype(f32))
        at(0, A[1][BEGIN])
        at(1, A[0][BEGIN], B[1][SCATTER], lambda: waits(bring_back))
        for i in range(n_tiles):
            attend_back_tile(R, l, i)
            if i == 1:
                at(0, A[1][SCATTER], lambda: starts(bring_back[:2]))
                at(1, A[0][SCATTER])
            if i == 2:
                at(1, A[1][SUM])
        at(0, lambda: starts(bring_back[2:]))
        at(1, B[1][SUM])
        project_back(R, l)
        at(0, lambda: start_din(1))
        at(1, lambda: start_din(0))
        weight_back(R, l)
        at(0, B[1][BEGIN])
        at(1, B[0][BEGIN])
        return 0

    lax.fori_loop(0, 2, backward, 0)

    B[0][SCATTER]()
    A[0][SUM]()
    A[1][GATHER]()
    B[1][GATHER]()
    A[0][GATHER]()
    B[0][SUM]()
    pl.when(sec == 1)(lambda: starts(din_away[1][2:]))
    A[1][SHARE]()
    B[1][SHARE]()
    B[0][GATHER]()
    A[0][SHARE]()
    A[1][FINISH]()
    B[1][FINISH]()
    B[0][SHARE]()
    A[0][FINISH]()
    B[0][FINISH]()

    for l in range(2):

        @pl.when(sec == l)
        def _():
            x_out[l][0].wait()
            x_out[1 - l][1].wait_send()
            x_out[l][1].wait_recv()
            if l == 0:
                din_local[0].wait()
                din_away[0].wait_send()
                for x in din_away[1]:
                    x.wait_recv()
            else:
                for x in din_away[1]:
                    x.wait_send()
                din_away[0].wait_recv()


def place(n, *refs):
    names = OUTS + ["layer", "grad", "gqkv", "gout", "gup", "gdown", "ggains", "gbias", "gupb", "d", "a", "b", "df", "af", "bf", "tf", "small", "lay", "sem"]
    R = types.SimpleNamespace(**dict(zip(names, refs)))
    sec = lax.axis_index("section")
    used = iter(range(16))
    copy = lambda src, dst: pltpu.make_async_copy(src, dst, R.sem.at[next(used)])
    loads = [copy(R.res_a, R.a), copy(R.res_b, R.b), copy(R.rdin, R.d), copy(R.small_out, R.small)]
    loads += [copy(R.din_own, R.df.at[sec]), copy(R.layer_out, R.lay)]
    for x in loads:
        x.start()

    def row(small, i):
        return jnp.concatenate([small[0, i : i + 1, :], small[1, i : i + 1, :]], axis=1)

    loads[3].wait()
    for i in range(2):
        R.ggains[0, i : i + 1, :] = row(R.small, i)
        R.gupb[0, :, 256 * i : 256 * i + 256] = row(R.small, 6 + i)
        R.gbias[i] = row(R.small, 8 + i)
    for i in range(2, 6):
        R.gbias[i] = row(R.small, i)
    loads[0].wait()
    R.af[...] = R.a[:, 0:768].astype(f32)
    out = [copy(R.af.at[:, pl.ds(0, 256)], R.gout.at[0]), copy(R.af.at[:, pl.ds(256, 512)], R.gup.at[0])]
    R.tf[...] = R.a[:, 768:1280].astype(f32).T
    out += [copy(R.tf, R.gdown.at[0])]
    for x in out:
        x.start()
    loads[1].wait()
    R.bf[...] = R.b[...].astype(f32)
    out += [copy(R.bf, R.gqkv.at[0])]
    out[-1].start()
    loads[2].wait()
    R.df[1 - sec] = R.d[...].astype(f32)
    loads[4].wait()
    out += [copy(R.df, R.grad.at[0])]
    out[-1].start()
    loads[5].wait()
    out += [copy(R.lay, R.layer.at[0])]
    out[-1].start()
    for x in out:
        x.wait()


def kernel_call(dp, n, lengths, segments, cells, ograd, *weights):
    chips = min(8, dp // 2)
    groups = dp // (2 * chips)
    sc = scratch(n, chips, groups)

    def kern(*refs):
        body(types.SimpleNamespace(**dict(zip(names, refs))), n, dp)

    stash = [(HEADS * TILE, width) for _, width in spans(n)]
    names = INS + OUTS + ["stash%d" % i for i in range(len(stash))] + list(sc)
    vmem, smem, anywhere = [pl.BlockSpec(memory_space=m) for m in (pltpu.VMEM, pltpu.SMEM, pl.ANY)]
    shapes = [((2, n, 256), bf16), ((n, 256), f32), ((n, 256), bf16), ((256, 1280), bf16), ((256, 768), bf16)]
    shapes += [((2, 16, 128), f32)] + [(s, bf16) for s in stash]
    parts = pl.pallas_call(
        kern,
        out_shape=[jax.ShapeDtypeStruct(*s) for s in shapes],
        in_specs=[smem, vmem] + [anywhere] * 9,
        out_specs=[anywhere] * (len(OUTS) + len(stash)),
        scratch_shapes=list(sc.values()),
        compiler_params=pltpu.CompilerParams(
            vmem_limit_bytes=62 * 2**20, collective_id=0, has_side_effects=True
        ),
    )(lengths, segments, cells, ograd, *weights)[: len(OUTS)]
    shapes = [((1, 2, n, 256), bf16), ((1, 2, n, 256), f32), ((1, 256, 768), f32), ((1, 256, 256), f32),
              ((1, 256, 512), f32), ((1, 512, 256), f32), ((1, 2, 256), f32), ((6, 1, 256), f32), ((1, 1, 512), f32)]
    return pl.pallas_call(
        lambda *refs: place(n, *refs),
        out_shape=[jax.ShapeDtypeStruct(*s) for s in shapes],
        in_specs=[anywhere] * len(OUTS),
        out_specs=[anywhere] * 6 + [vmem] * 3,
        scratch_shapes=[
            pltpu.VMEM((n, 256), bf16), pltpu.VMEM((256, 1280), bf16), pltpu.VMEM((256, 768), bf16),
            pltpu.VMEM((2, n, 256), f32), pltpu.VMEM((256, 768), f32), pltpu.VMEM((256, 768), f32), pltpu.VMEM((512, 256), f32),
            pltpu.VMEM((2, 16, 128), f32), pltpu.VMEM((2, n, 256), bf16),
            pltpu.SemaphoreType.DMA((16,)),
        ],
        compiler_params=pltpu.CompilerParams(vmem_limit_bytes=62 * 2**20),
    )(*parts)


def solution(mesh):
    dp = mesh.shape["dp"]

    def on_device(cells, ograd, segments, lengths, *weights):
        *matrices, biases, up = weights
        weights = (*matrices, biases.transpose(1, 0, 2), up[:, None, :])
        out = kernel_call(dp, cells.shape[1], lengths, segments, cells, ograd, *weights)
        return (*out[:7], out[7].transpose(1, 0, 2), out[8][:, 0, :])

    w3, w2 = P("section", None, None), P("section", None)
    rows = P("section", "dp", None, None)
    return jax.shard_map(
        on_device,
        mesh=mesh,
        in_specs=(P("dp", None, None), P("dp", None, None), P("dp", None), P("dp"), w3, w3, w3, w3, w3, w3, w2),
        out_specs=(rows, rows, w3, w3, w3, w3, w3, w3, w2),
        check_vma=False,
    )
```

profile of v0, /device:TPU:0, one launch (start us, length us, event | category | flops | bytes accessed | tf_op | source)
XLA Modules:
  0.0 98.9 jit_solution(7462527079995924971)
XLA Ops:
  0.6 93.6 %shard_map.178 = (bf16[2,1024,256]{2,1,0:T(8,128)(2,1)}, f32[1024,256]{1,0:T(8,128)}, bf16[1024,256]{1,0:T(8,128)(2,1)}, bf16[256,1280]{1,0:T(8,128)(2,1)}, bf16...) custom-call(s32[2]{0:T(128)} %refs_0_.1, ...), custom_call_target="tpu_custom_call" | custom-call | tf_op jit(solution)/shard_map/pallas_call | solution.py:698
  94.3 4.4 %shard_map.179 = (bf16[1,2,1024,256]{3,2,1,0:T(8,128)(2,1)}, f32[1,2,1024,256]{3,2,1,0:T(8,128)}, f32[1,256,768]{2,1,0:T(8,128)}, f32[1,256,256]{2,1,0:T(8,128)}...) custom-call(bf16[2,1024,256]{2,1,0:T(8,128)(2,1)} %get-tuple-element, ...), custom_call_target="tpu_custom_call" | custom-call | tf_op jit(solution)/shard_map/pallas_call | solution.py:710
where the time goes:
time: 99.1 us; the launch traced here: 98.9 us
  Pallas kernels  98.1 us (99%)
    pallas_call x1, Pallas kernels, kernel_call(): pl.pallas_call(kern, out_shape=[jax.ShapeDtypeStruct(*s) for s in shapes]...  93.6 us
    pallas_call x1, Pallas kernels, kernel_call(): pl.pallas_call(lambda *refs: place(n, *refs), out_shape=[jax.ShapeDtypeSt...  4.43 us

commit v1 on v0

--- a/solution.py
+++ b/solution.py
@@ -190,22 +190,29 @@
     R.grad_a[l, :, 0:256] = dot_tn(R.octx[l].astype(bf16), R.datt[...])
     R.grad_a[l, :, 256:768] = dot_tn(low, R.dup[...])
     R.grad_a[l, :, 768:1280] = dot_tn(R.dlow[...], R.act[l])
-    R.dkT[...] = jnp.zeros_like(R.dkT)
-    R.dvT[...] = jnp.zeros_like(R.dvT)
+
+
+def add_columns(ref, head, lo, begun, v):
+    old = max(0, min(begun - lo, v.shape[1]))
+    if old:
+        ref[head, pl.ds(lo, old)] += v[:, 0:old]
+    if old < v.shape[1]:
+        ref[head, pl.ds(lo + old, v.shape[1] - old)] = v[:, old:]
 
 
 def attend_back_tile(R, l, i):
     lo, width = spans(R.n)[i]
+    begun = max([a + b for a, b in spans(R.n)[:i]], default=0)
     rows, cols = pl.ds(i * TILE, TILE), pl.ds(lo, width)
     for h in range(HEADS):
         head, part = slice(64 * h, 64 * h + 64), slice(h * TILE, h * TILE + TILE)
         p = R.P[i][part, :]
         dp = dot(R.doh[h, rows, :], R.vT[64 * h : 64 * h + 128, cols])
         R.DS[part, 0:width] = (p.astype(f32) * (dp - R.delta[rows, h : h + 1])).astype(bf16)
-        R.dvT[head, cols] += dot(R.doT[head, rows], p)
+        add_columns(R.dvT, head, lo, begun, dot(R.doT[head, rows], p))
     for h in range(HEADS):
         head, part = slice(64 * h, 64 * h + 64), slice(h * TILE, h * TILE + TILE)
-        R.dkT[head, cols] += dot(R.qT[head, rows], R.DS[part, 0:width])
+        add_columns(R.dkT, head, lo, begun, dot(R.qT[head, rows], R.DS[part, 0:width]))
     R.dqkv[rows, 0:256] = (pick_heads(dot(R.DS[:, 0:width], R.kn[l, cols, :])) * 0.125).astype(bf16)
 
 
@@ -280,120 +287,144 @@
         return pltpu.make_async_copy(src, dst, self.local_sem.at[i])
 
 
-def reduction(K, l, grad, small, R, name):
+def reduction(K, l, grad, small, R, name, sum_two, give_two):
     get = lambda part: getattr(R, name + "_" + part).at[l]
-    r1, s2, r2, acc, r3, done = [get(p) for p in ("r1", "s2", "r2", "acc", "r3", "done")]
-    res = getattr(R, "res_" + name)
+    r1, s2, ry, r2, acc, r3 = [get(p) for p in ("r1", "s2", "ry", "r2", "acc", "r3")]
+    res, out = getattr(R, name + "_res"), getattr(R, "res_" + name)
     c, chip, chips, groups = K.core, K.chip, K.chips, K.groups
     half = grad.shape[0] // 2
     piece = half // chips
-    mine = pl.ds(c * half, half)
-    other = pl.ds((1 - c) * half, half)
-    part = pl.ds(c * half + chip * piece, piece)
+    near = half // 2
+    line = chips // 2
+
+    def place_of(index):
+        return (index % 2) * near + (index // 2) * piece
+
+    start = c * half
+    mine, other = pl.ds(start, half), pl.ds((1 - c) * half, half)
+    my_near, other_near = (chip % 2) * near, (1 - chip % 2) * near
+    part = pl.ds(place_of(chip), piece)
     owner = K.sec == l
+    has_small = small is not None
     core_out = [K.remote(grad.at[other], r1, K.core_peer())]
-    scatter = []
-    for k in range(1, chips):
-        there = K.xor(chip, k)
-        scatter.append(K.remote(s2.at[pl.ds(there * piece, piece)], r2.at[k], K.chip_peer(k)))
+    everyone = range(1, chips)
+    ahead = range(2, chips, 2)
+    to_near = [K.remote(s2.at[pl.ds(other_near, near)], ry, K.chip_peer(1))] if sum_two else []
+    targets = ahead if sum_two else everyone
+    scatter = [
+        K.remote(s2.at[pl.ds(place_of(K.xor(chip, k)), piece)], r2.at[k], K.chip_peer(k)) for k in targets
+    ]
     across = [K.remote(acc, r3, K.section_peer())]
-    gather = [K.remote(done, res.at[part], K.chip_peer(k)) for k in range(1, chips)]
-    keep = K.local(done, res.at[part])
-    core_back = [K.remote(res.at[mine], res.at[mine], K.core_peer())]
     spread = []
     if groups > 1:
         r4 = get("r4")
         spread = [K.remote(acc, r4.at[k], K.group_peer(k)) for k in range(1, groups)]
-    if small is not None:
-        q1, q2, t2, qacc, q3, qres = [get(p) for p in ("q1", "q2", "t2", "qacc", "q3", "qres")]
+    gather = [
+        K.remote(res.at[part], res.at[part], K.chip_peer(k)) for k in (ahead if give_two else everyone)
+    ]
+    rows = pl.ds(my_near, near)
+    from_near = [K.remote(res.at[rows], res.at[rows], K.chip_peer(1))] if give_two else []
+    core_back = [K.remote(res, out.at[mine], K.core_peer())]
+    keep = [K.local(res, out.at[mine])]
+    if has_small:
+        q1, q2, ty, t2, qacc, q3, qres = [get(p) for p in ("q1", "q2", "ty", "t2", "qacc", "q3", "qres")]
         core_out.append(K.remote(small.at[1 - c], q1, K.core_peer()))
-        scatter += [K.remote(q2, t2.at[k], K.chip_peer(k)) for k in range(1, chips)]
-        across.append(K.remote(qacc, q3, K.section_peer()))
-        core_back.append(K.remote(qres.at[c], qres.at[c], K.core_peer()))
-        small_out = K.local(qres, R.small_out)
+        if sum_two:
+            to_near.append(K.remote(q2, ty, K.chip_peer(1)))
+        little_src = qacc if sum_two else q2
+        scatter += [K.remote(little_src, t2.at[k], K.chip_peer(k)) for k in targets]
+        across.append(K.remote(q2, q3, K.section_peer()))
+        core_back.append(K.remote(qres, R.small_out.at[c], K.core_peer()))
+        keep.append(K.local(qres, R.small_out.at[c]))
         if groups > 1:
             q4 = get("q4")
             spread += [K.remote(qacc, q4.at[k], K.group_peer(k)) for k in range(1, groups)]
 
+    def each(copies, *what):
+        for w in what:
+            for x in copies:
+                getattr(x, w)()
+
     def begin():
-        for x in core_out:
-            x.start()
-
-    def scatter_pieces():
-        for x in core_out:
-            x.wait()
+        each(core_out, "start")
+
+    def to_neighbour():
+        each(core_out, "wait")
         total = grad[mine, :] + r1[...]
         grad[mine, :] = total
         s2[...] = total.astype(bf16)
-        if small is not None:
+        if has_small:
             q2[...] = small[c] + q1[...]
-        for x in scatter:
-            x.start()
+        each(to_near if sum_two else scatter, "start")
+
+    def to_line():
+        if sum_two:
+            each(to_near, "wait")
+            own = pl.ds(start + my_near, near)
+            total = grad[own, :] + ry[...].astype(f32)
+            grad[own, :] = total
+            s2[pl.ds(my_near, near), :] = total.astype(bf16)
+            if has_small:
+                qacc[...] = q2[...] + ty[...]
+            each(scatter, "start")
 
     def sum_pieces():
-        for x in scatter:
-            x.wait()
-        total = grad[part, :]
-        for k in range(1, chips):
+        each(scatter, "wait")
+        total = grad[pl.ds(start + place_of(chip), piece), :]
+        for k in targets:
             total = total + r2[k].astype(f32)
         acc[...] = total
-        if small is not None:
-            little = q2[...]
-            for k in range(1, chips):
+        if has_small:
+            little = little_src[...]
+            for k in targets:
                 little = little + t2[k]
-            qacc[...] = little
-
-        @pl.when(jnp.logical_not(owner))
-        def _():
-            for x in across:
-                x.start()
-            for x in across:
-                x.wait_send()
-
-    def gather_pieces():
+            q2[...] = little
+        pl.when(jnp.logical_not(owner))(lambda: each(across, "start", "wait_send"))
+
+    def give_line():
         @pl.when(owner)
         def _():
-            for x in across:
-                x.wait_recv()
+            each(across, "wait_recv")
             acc[...] += r3[...]
-            if small is not None:
-                qacc[...] += q3[...]
-            for x in spread:
-                x.start()
-            for x in spread:
-                x.wait()
+            if has_small:
+                qacc[...] = q2[...] + q3[...]
+            each(spread, "start", "wait")
             total = acc[...]
             for k in range(1, groups):
                 total = total + r4[k]
-            done[...] = total.astype(bf16)
-            for x in gather:
-                x.start()
-            keep.start()
-            if small is not None:
+            res[part, :] = total.astype(bf16)
+            each(gather, "start")
+            if has_small:
                 little = qacc[...]
                 for k in range(1, groups):
                     little = little + q4[k]
-                qres[c] = little
-                core_back[1].start()
+                qres[...] = little
+
+    def give_neighbour():
+        if give_two:
+
+            @pl.when(owner)
+            def _():
+                each(gather, "wait")
+                each(from_near, "start")
 
     def share():
         @pl.when(owner)
         def _():
-            for x in gather:
-                x.wait()
-            keep.wait()
-            core_back[0].start()
+            each(from_near if give_two else gather, "wait")
+            each(core_back, "start")
+            each(keep, "start")
 
     def finish():
         @pl.when(owner)
         def _():
-            for x in core_back:
-                x.wait()
-            if small is not None:
-                small_out.start()
-                small_out.wait()
-
-    return begin, scatter_pieces, sum_pieces, gather_pieces, share, finish
+            each(core_back, "wait")
+            each(keep, "wait")
+
+    return begin, to_neighbour, to_line, sum_pieces, give_line, give_neighbour, share, finish
+
+
+TWO = ((False, False), (False, True), (False, False), (False, True))
 
 
 def scratch(n, chips, groups):
@@ -423,10 +454,11 @@
         out[name + "_r2"] = V(2, chips, piece, width, bf16)
         out[name + "_acc"] = V(2, piece, width, f32)
         out[name + "_r3"] = V(2, piece, width, f32)
-        out[name + "_done"] = V(2, piece, width, bf16)
+        out[name + "_ry"] = V(2, 64, width, bf16)
+        out[name + "_res"] = V(128, width, bf16)
         if groups > 1:
             out[name + "_r4"] = V(2, groups, piece, width, f32)
-    for part, lead in (("q1", ()), ("q2", ()), ("t2", (chips,)), ("qacc", ()), ("q3", ()), ("qres", (2,)), ("q4", (groups,))):
+    for part, lead in (("q1", ()), ("q2", ()), ("ty", ()), ("t2", (chips,)), ("qacc", ()), ("q3", ()), ("qres", ()), ("q4", (groups,))):
         out["b_" + part] = V(2, *lead, 16, 128, f32)
     for i, (_, width) in enumerate(spans(n)):
         out["P%d" % i] = V(HEADS * TILE, width, bf16)
@@ -550,9 +582,9 @@
     lax.fori_loop(0, 2, forward, 0)
 
     R.small[...] = jnp.zeros_like(R.small)
-    A = [reduction(K, l, R.grad_a.at[l], None, R, "a") for l in range(2)]
-    B = [reduction(K, l, R.grad_b.at[l], R.small.at[l], R, "b") for l in range(2)]
-    BEGIN, SCATTER, SUM, GATHER, SHARE, FINISH = range(6)
+    A = [reduction(K, l, R.grad_a.at[l], None, R, "a", TWO[0][l], TWO[1][l]) for l in range(2)]
+    B = [reduction(K, l, R.grad_b.at[l], R.small.at[l], R, "b", TWO[2][l], TWO[3][l]) for l in range(2)]
+    BEGIN, NEAR, LINE, SUM, GIVE, GIVE_NEAR, SHARE, FINISH = range(8)
 
     din_local = [K.local(R.d1, R.din_own) for l in range(2)]
     quarter = n // 4
@@ -583,16 +615,15 @@
         at(1, lambda: pl.when(sec == 1)(din_local[1].wait))
         feed_back(R, l, R.dinb[j].astype(f32))
         at(0, A[1][BEGIN])
-        at(1, A[0][BEGIN], B[1][SCATTER], lambda: waits(bring_back))
+        at(1, A[0][BEGIN], A[1][LINE], B[1][NEAR], lambda: waits(bring_back))
         for i in range(n_tiles):
             attend_back_tile(R, l, i)
             if i == 1:
-                at(0, A[1][SCATTER], lambda: starts(bring_back[:2]))
-                at(1, A[0][SCATTER])
+                at(0, A[1][NEAR], lambda: starts(bring_back[:2]))
+                at(1, A[0][NEAR])
             if i == 2:
-                at(1, A[1][SUM])
+                at(1, B[1][LINE])
         at(0, lambda: starts(bring_back[2:]))
-        at(1, B[1][SUM])
         project_back(R, l)
         at(0, lambda: start_din(1))
         at(1, lambda: start_din(0))
@@ -603,20 +634,28 @@
 
     lax.fori_loop(0, 2, backward, 0)
 
-    B[0][SCATTER]()
+    A[0][LINE]()
+    B[0][NEAR]()
     A[0][SUM]()
-    A[1][GATHER]()
-    B[1][GATHER]()
-    A[0][GATHER]()
+    A[1][SUM]()
+    B[1][SUM]()
+    B[0][LINE]()
+    A[0][GIVE]()
     B[0][SUM]()
     pl.when(sec == 1)(lambda: starts(din_away[1][2:]))
+    A[1][GIVE]()
+    B[1][GIVE]()
+    B[0][GIVE]()
+    A[0][GIVE_NEAR]()
+    A[1][GIVE_NEAR]()
+    B[1][GIVE_NEAR]()
+    B[0][GIVE_NEAR]()
+    A[0][SHARE]()
     A[1][SHARE]()
     B[1][SHARE]()
-    B[0][GATHER]()
-    A[0][SHARE]()
+    B[0][SHARE]()
     A[1][FINISH]()
     B[1][FINISH]()
-    B[0][SHARE]()
     A[0][FINISH]()
     B[0][FINISH]()
 

time: 99.1 us -> 95.5 us (0.964)
  Pallas kernels: 98.1 us -> 93.6 us
    pallas_call x1, Pallas kernels: 93.6 us -> 89.2 us  [kernel_call(): pl.pallas_call(kern, out_shape=[jax.ShapeDtypeStruct(*s) for s in shapes]...]
where the time goes in v1:
time: 95.5 us; the launch traced here: 94.4 us
  Pallas kernels  93.6 us (98%)
    pallas_call x1, Pallas kernels, kernel_call(): pl.pallas_call(kern, out_shape=[jax.ShapeDtypeStruct(*s) for s in shapes]...  89.2 us
    pallas_call x1, Pallas kernels, kernel_call(): pl.pallas_call(lambda *refs: place(n, *refs), out_shape=[jax.ShapeDtypeSt...  4.43 us

profile of v1, /device:TPU:0, one launch (start us, length us, event | category | flops | bytes accessed | tf_op | source)
XLA Modules:
  0.0 94.4 jit_solution(2221091457127533946)
XLA Ops:
  0.6 89.2 %shard_map.178 = (bf16[2,1024,256]{2,1,0:T(8,128)(2,1)}, f32[1024,256]{1,0:T(8,128)}, bf16[1024,256]{1,0:T(8,128)(2,1)}, bf16[256,1280]{1,0:T(8,128)(2,1)}, bf16...) custom-call(s32[2]{0:T(128)} %refs_0_.1, ...), custom_call_target="tpu_custom_call" | custom-call | tf_op jit(solution)/shard_map/pallas_call | solution.py:737
  89.8 4.4 %shard_map.179 = (bf16[1,2,1024,256]{3,2,1,0:T(8,128)(2,1)}, f32[1,2,1024,256]{3,2,1,0:T(8,128)}, f32[1,256,768]{2,1,0:T(8,128)}, f32[1,256,256]{2,1,0:T(8,128)}...) custom-call(bf16[2,1024,256]{2,1,0:T(8,128)(2,1)} %get-tuple-element, ...), custom_call_target="tpu_custom_call" | custom-call | tf_op jit(solution)/shard_map/pallas_call | solution.py:749

commit v2 on v1

--- a/solution.py
+++ b/solution.py
@@ -175,6 +175,14 @@
     R.datt[...] = da
     dcb = dot(da, R.woutT[...]).astype(bf16)
     R.dctx[...] = dcb
+    R.grad_a[l, :, 0:256] = dot_tn(R.octx[l].astype(bf16), R.datt[...])
+    R.grad_a[l, :, 256:768] = dot_tn(low, R.dup[...])
+    R.grad_a[l, :, 768:1280] = dot_tn(R.dlow[...], R.act[l])
+
+
+def attend_prepare(R, l):
+    n = R.n
+    dcb = R.dctx[...]
     dc = dcb.astype(f32)
     e = dc * R.octx[l]
     lane = lanes(n)
@@ -187,9 +195,6 @@
     R.doT[...] = dcb.T
     R.qT[...] = R.qn[l].T
     R.vT[0:256, :] = R.vn[l].T
-    R.grad_a[l, :, 0:256] = dot_tn(R.octx[l].astype(bf16), R.datt[...])
-    R.grad_a[l, :, 256:768] = dot_tn(low, R.dup[...])
-    R.grad_a[l, :, 768:1280] = dot_tn(R.dlow[...], R.act[l])
 
 
 def add_columns(ref, head, lo, begun, v):
@@ -379,7 +384,7 @@
             for k in targets:
                 little = little + t2[k]
             q2[...] = little
-        pl.when(jnp.logical_not(owner))(lambda: each(across, "start", "wait_send"))
+        pl.when(jnp.logical_not(owner))(lambda: each(across, "start"))
 
     def give_line():
         @pl.when(owner)
@@ -420,6 +425,8 @@
         def _():
             each(core_back, "wait")
             each(keep, "wait")
+
+        pl.when(jnp.logical_not(owner))(lambda: each(across, "wait_send"))
 
     return begin, to_neighbour, to_line, sum_pieces, give_line, give_neighbour, share, finish
 
@@ -486,7 +493,7 @@
     R.seg_row = R.seg_v[pl.ds(sec, 1), :]
 
     barrier = pltpu.get_barrier_semaphore()
-    peers = K.peers()
+    peers = K.peers()[::-1]
     for peer in peers:
         pl.semaphore_signal(barrier, 1, device_id=peer, device_id_type=MESH)
 
@@ -616,6 +623,7 @@
         feed_back(R, l, R.dinb[j].astype(f32))
         at(0, A[1][BEGIN])
         at(1, A[0][BEGIN], A[1][LINE], B[1][NEAR], lambda: waits(bring_back))
+        attend_prepare(R, l)
         for i in range(n_tiles):
             attend_back_tile(R, l, i)
             if i == 1:
@@ -683,40 +691,44 @@
     sec = lax.axis_index("section")
     used = iter(range(16))
     copy = lambda src, dst: pltpu.make_async_copy(src, dst, R.sem.at[next(used)])
-    loads = [copy(R.res_a, R.a), copy(R.res_b, R.b), copy(R.rdin, R.d), copy(R.small_out, R.small)]
-    loads += [copy(R.din_own, R.df.at[sec]), copy(R.layer_out, R.lay)]
-    for x in loads:
+    lay, own, far, low_a, low_b, low = [
+        copy(R.layer_out, R.lay), copy(R.din_own, R.df.at[sec]), copy(R.rdin, R.d),
+        copy(R.res_a, R.a), copy(R.res_b, R.b), copy(R.small_out, R.small),
+    ]
+    for x in (lay, own, far, low_a, low_b, low):
         x.start()
+    out = [
+        copy(R.lay, R.layer.at[0]), copy(R.df.at[sec], R.grad.at[0, sec]), copy(R.df.at[1 - sec], R.grad.at[0, 1 - sec]),
+        copy(R.af.at[:, pl.ds(0, 256)], R.gout.at[0]), copy(R.af.at[:, pl.ds(256, 512)], R.gup.at[0]),
+        copy(R.tf, R.gdown.at[0]), copy(R.bf, R.gqkv.at[0]),
+    ]
+    lay.wait()
+    out[0].start()
+    own.wait()
+    out[1].start()
+    far.wait()
+    R.df[1 - sec] = R.d[...].astype(f32)
+    out[2].start()
+    low_a.wait()
+    R.af[...] = R.a[:, 0:768].astype(f32)
+    out[3].start()
+    out[4].start()
+    R.tf[...] = R.a[:, 768:1280].astype(f32).T
+    out[5].start()
+    low_b.wait()
+    R.bf[...] = R.b[...].astype(f32)
+    out[6].start()
+    low.wait()
 
     def row(small, i):
         return jnp.concatenate([small[0, i : i + 1, :], small[1, i : i + 1, :]], axis=1)
 
-    loads[3].wait()
     for i in range(2):
         R.ggains[0, i : i + 1, :] = row(R.small, i)
         R.gupb[0, :, 256 * i : 256 * i + 256] = row(R.small, 6 + i)
         R.gbias[i] = row(R.small, 8 + i)
     for i in range(2, 6):
         R.gbias[i] = row(R.small, i)
-    loads[0].wait()
-    R.af[...] = R.a[:, 0:768].astype(f32)
-    out = [copy(R.af.at[:, pl.ds(0, 256)], R.gout.at[0]), copy(R.af.at[:, pl.ds(256, 512)], R.gup.at[0])]
-    R.tf[...] = R.a[:, 768:1280].astype(f32).T
-    out += [copy(R.tf, R.gdown.at[0])]
-    for x in out:
-        x.start()
-    loads[1].wait()
-    R.bf[...] = R.b[...].astype(f32)
-    out += [copy(R.bf, R.gqkv.at[0])]
-    out[-1].start()
-    loads[2].wait()
-    R.df[1 - sec] = R.d[...].astype(f32)
-    loads[4].wait()
-    out += [copy(R.df, R.grad.at[0])]
-    out[-1].start()
-    loads[5].wait()
-    out += [copy(R.lay, R.layer.at[0])]
-    out[-1].start()
     for x in out:
         x.wait()
 

time: 95.5 us -> 93.2 us (0.976)
  Pallas kernels: 93.6 us -> 92.1 us
    pallas_call x1, Pallas kernels: 89.2 us -> 87.8 us  [kernel_call(): pl.pallas_call(kern, out_shape=[jax.ShapeDtypeStruct(*s) for s in shapes]...]
where the time goes in v2:
time: 93.2 us; the launch traced here: 92.9 us
  Pallas kernels  92.1 us (99%)
    pallas_call x1, Pallas kernels, kernel_call(): pl.pallas_call(kern, out_shape=[jax.ShapeDtypeStruct(*s) for s in shapes]...  87.8 us
    pallas_call x1, Pallas kernels, kernel_call(): pl.pallas_call(lambda *refs: place(n, *refs), out_shape=[jax.ShapeDtypeSt...  4.31 us

profile of v2, /device:TPU:0, one launch (start us, length us, event | category | flops | bytes accessed | tf_op | source)
XLA Modules:
  0.0 92.9 jit_solution(11204363833801607251)
XLA Ops:
  0.6 87.8 %shard_map.178 = (bf16[2,1024,256]{2,1,0:T(8,128)(2,1)}, f32[1024,256]{1,0:T(8,128)}, bf16[1024,256]{1,0:T(8,128)(2,1)}, bf16[256,1280]{1,0:T(8,128)(2,1)}, bf16...) custom-call(s32[2]{0:T(128)} %refs_0_.1, ...), custom_call_target="tpu_custom_call" | custom-call | tf_op jit(solution)/shard_map/pallas_call | solution.py:749
  88.5 4.3 %shard_map.179 = (bf16[1,2,1024,256]{3,2,1,0:T(8,128)(2,1)}, f32[1,2,1024,256]{3,2,1,0:T(8,128)}, f32[1,256,768]{2,1,0:T(8,128)}, f32[1,256,256]{2,1,0:T(8,128)}...) custom-call(bf16[2,1024,256]{2,1,0:T(8,128)(2,1)} %get-tuple-element, ...), custom_call_target="tpu_custom_call" | custom-call | tf_op jit(solution)/shard_map/pallas_call | solution.py:761

commit v3 on v2

--- a/solution.py
+++ b/solution.py
@@ -431,7 +431,7 @@
     return begin, to_neighbour, to_line, sum_pieces, give_line, give_neighbour, share, finish
 
 
-TWO = ((False, False), (False, True), (False, False), (False, True))
+TWO = ((False, False), (True, True), (False, False), (False, True))
 
 
 def scratch(n, chips, groups):

time: 93.2 us -> 92.9 us (level)
  Pallas kernels: 92.1 us -> 91.1 us
    pallas_call x1, Pallas kernels: 87.8 us -> 86.8 us  [kernel_call(): pl.pallas_call(kern, out_shape=[jax.ShapeDtypeStruct(*s) for s in shapes]...]
where the time goes in v3:
time: 92.9 us; the launch traced here: 91.9 us
  Pallas kernels  91.1 us (98%)
    pallas_call x1, Pallas kernels, kernel_call(): pl.pallas_call(kern, out_shape=[jax.ShapeDtypeStruct(*s) for s in shapes]...  86.8 us
    pallas_call x1, Pallas kernels, kernel_call(): pl.pallas_call(lambda *refs: place(n, *refs), out_shape=[jax.ShapeDtypeSt...  4.31 us

profile of v3, /device:TPU:0, one launch (start us, length us, event | category | flops | bytes accessed | tf_op | source)
XLA Modules:
  0.0 91.9 jit_solution(11322105638811747963)
XLA Ops:
  0.6 86.8 %shard_map.178 = (bf16[2,1024,256]{2,1,0:T(8,128)(2,1)}, f32[1024,256]{1,0:T(8,128)}, bf16[1024,256]{1,0:T(8,128)(2,1)}, bf16[256,1280]{1,0:T(8,128)(2,1)}, bf16...) custom-call(s32[2]{0:T(128)} %refs_0_.1, ...), custom_call_target="tpu_custom_call" | custom-call | tf_op jit(solution)/shard_map/pallas_call | solution.py:749
  87.5 4.3 %shard_map.179 = (bf16[1,2,1024,256]{3,2,1,0:T(8,128)(2,1)}, f32[1,2,1024,256]{3,2,1,0:T(8,128)}, f32[1,256,768]{2,1,0:T(8,128)}, f32[1,256,256]{2,1,0:T(8,128)}...) custom-call(bf16[2,1024,256]{2,1,0:T(8,128)(2,1)} %get-tuple-element, ...), custom_call_target="tpu_custom_call" | custom-call | tf_op jit(solution)/shard_map/pallas_call | solution.py:761

commit v4 on v3

--- a/solution.py
+++ b/solution.py
@@ -354,7 +354,7 @@
         each(core_out, "start")
 
     def to_neighbour():
-        each(core_out, "wait")
+        each(core_out, "wait_recv")
         total = grad[mine, :] + r1[...]
         grad[mine, :] = total
         s2[...] = total.astype(bf16)
@@ -374,49 +374,56 @@
             each(scatter, "start")
 
     def sum_pieces():
-        each(scatter, "wait")
+        each(scatter[: len(targets)], "wait_recv")
         total = grad[pl.ds(start + place_of(chip), piece), :]
         for k in targets:
             total = total + r2[k].astype(f32)
         acc[...] = total
+        pl.when(jnp.logical_not(owner))(across[0].start)
         if has_small:
+            each(scatter[len(targets) :], "wait")
             little = little_src[...]
             for k in targets:
                 little = little + t2[k]
             q2[...] = little
-        pl.when(jnp.logical_not(owner))(lambda: each(across, "start"))
+            pl.when(jnp.logical_not(owner))(across[1].start)
 
     def give_line():
         @pl.when(owner)
         def _():
-            each(across, "wait_recv")
+            across[0].wait_recv()
             acc[...] += r3[...]
-            if has_small:
-                qacc[...] = q2[...] + q3[...]
-            each(spread, "start", "wait")
+            if groups > 1:
+                if has_small:
+                    across[1].wait_recv()
+                    qacc[...] = q2[...] + q3[...]
+                each(spread, "start", "wait")
             total = acc[...]
             for k in range(1, groups):
                 total = total + r4[k]
             res[part, :] = total.astype(bf16)
             each(gather, "start")
-            if has_small:
+            if has_small and groups > 1:
                 little = qacc[...]
                 for k in range(1, groups):
                     little = little + q4[k]
                 qres[...] = little
+            elif has_small:
+                across[1].wait_recv()
+                qres[...] = q2[...] + q3[...]
 
     def give_neighbour():
         if give_two:
 
             @pl.when(owner)
             def _():
-                each(gather, "wait")
+                each(gather, "wait_recv")
                 each(from_near, "start")
 
     def share():
         @pl.when(owner)
         def _():
-            each(from_near if give_two else gather, "wait")
+            each(from_near if give_two else gather, "wait_recv")
             each(core_back, "start")
             each(keep, "start")
 
@@ -425,6 +432,9 @@
         def _():
             each(core_back, "wait")
             each(keep, "wait")
+            each(gather + from_near, "wait_send")
+
+        each(core_out + scatter[: len(targets)], "wait_send")
 
         pl.when(jnp.logical_not(owner))(lambda: each(across, "wait_send"))
 

time: 92.9 us -> 92.9 us (level)
  no operation moved by 1% of the time
where the time goes in v4:
time: 92.9 us; the launch traced here: 92.5 us
  Pallas kernels  91.7 us (99%)
    pallas_call x1, Pallas kernels, kernel_call(): pl.pallas_call(kern, out_shape=[jax.ShapeDtypeStruct(*s) for s in shapes]...  87.4 us
    pallas_call x1, Pallas kernels, kernel_call(): pl.pallas_call(lambda *refs: place(n, *refs), out_shape=[jax.ShapeDtypeSt...  4.31 us

profile of v4, /device:TPU:0, one launch (start us, length us, event | category | flops | bytes accessed | tf_op | source)
XLA Modules:
  0.0 92.5 jit_solution(4250200418861974630)
XLA Ops:
  0.6 87.4 %shard_map.178 = (bf16[2,1024,256]{2,1,0:T(8,128)(2,1)}, f32[1024,256]{1,0:T(8,128)}, bf16[1024,256]{1,0:T(8,128)(2,1)}, bf16[256,1280]{1,0:T(8,128)(2,1)}, bf16...) custom-call(s32[2]{0:T(128)} %refs_0_.1, ...), custom_call_target="tpu_custom_call" | custom-call | tf_op jit(solution)/shard_map/pallas_call | solution.py:759
  88.0 4.3 %shard_map.179 = (bf16[1,2,1024,256]{3,2,1,0:T(8,128)(2,1)}, f32[1,2,1024,256]{3,2,1,0:T(8,128)}, f32[1,256,768]{2,1,0:T(8,128)}, f32[1,256,256]{2,1,0:T(8,128)}...) custom-call(bf16[2,1024,256]{2,1,0:T(8,128)(2,1)} %get-tuple-element, ...), custom_call_target="tpu_custom_call" | custom-call | tf_op jit(solution)/shard_map/pallas_call | solution.py:771
